TPU v7x, 32 devices: a whole 2x2x4 slice. The times are simulated.
32 devices in a mesh: seg: 4 (over x, core), chan: 8 (over z, y).
Axes of the slice: x: 2, y: 2, z: 4, core: 2. Of those that a mesh axis runs over, the one named last changes fastest.
Arguments:
- traces: bfloat16 [32, 1024, 4096], P('seg', 'chan'), may hold values from -6 to 6
- channel_mask: int32 [1024], P('chan'), may hold values 0 or 1
- owner_ids: int32 [8, 64, 1], P('chan'), may hold values from 0 to 7; in each aligned block of 64 rows (0 to 63, 64 to 127, ..., all dimensions but the last counted through in order) at most 16 rows name the same one
- local_bins: int32 [8, 64], P('chan'), may hold values from 0 to 7
Outputs:
- stacks: float32 [64, 2048], P('chan')
Inputs may be any that keep to these rules, and one draw needn't show every extreme that they name: `owner_ids`: among the 64 tiles of one block no owner is named more than 16 times, a bound that some block reaches.
All inputs are finite; a program needn't handle non-finite values. No bound on the sum of `channel_mask` on one device may be relied on, other than what follows from the above.
Results may differ from a plain program's by a relative error of at most 0.0053.
Values may be sent and summed in bfloat16 or wider, within the bound.
No kernel may reach another device: no remote copies, remote signals or barrier semaphores. Data moves between devices by JAX's collectives and lax.ppermute only.
A program may use at most 192 MiB of HBM per device.

v0:
```python
import functools
import math

import jax
import jax.numpy as jnp
import ml_dtypes
import numpy as np
from jax import lax
from jax.experimental import pallas as pl
from jax.experimental.pallas import tpu as pltpu
from jax.sharding import PartitionSpec as P

NT = 4096
DEC = 2
K0 = 8
HW = 64
R = 4
G = 16
BIN_DEV = 8
NB = 1024
NLAG = 2048
EPSILON = 1e-06

LANES = 128
SLICES = NB // LANES
FOLD = 4
CLASS = NB // FOLD
QUARTER = NT // FOLD
LAGQ = NLAG // FOLD
VMEM = 58 * 1024 * 1024
VMEM_SMALL = 20 * 1024 * 1024
META = 16
PAIR = 2 * LANES
TIERS = (104, 8, 16)
KEPT = 2 * TIERS[0]
EARLY_SEGS = 2

SENT = (4, 1, 7, 3, 5, 2, 6)
STAGES = (6, 8)


ORDER = np.arange(NB).reshape(LANES, 2, FOLD).transpose(2, 1, 0).reshape(-1)
EIGHTH = NT // (2 * FOLD)


def forward_tables():
    samples = np.arange(QUARTER, dtype=np.int64)
    freqs = K0 + ORDER.astype(np.int64)
    phase = samples[:, None] * freqs[None, :] % NT
    angle = (phase.astype(np.float32) * np.float32(2.0 * math.pi / NT)).astype(np.float64)
    cos = np.cos(angle).astype(np.float32).astype(ml_dtypes.bfloat16)
    sin = (-np.sin(angle)).astype(np.float32).astype(ml_dtypes.bfloat16)

    def part(which, rows, half=slice(0, CLASS)):
        columns = slice(which * CLASS + half.start, which * CLASS + half.stop)
        return [cos[:rows, columns], sin[:rows, columns]]

    halves = [part(0, EIGHTH, slice(at, at + LANES)) for at in (0, LANES)]
    zero, two = np.concatenate(halves[0] + halves[1], axis=1), np.concatenate(part(2, EIGHTH), axis=1)
    odd = np.concatenate(part(1, QUARTER) + part(3, QUARTER), axis=1)
    return np.stack([zero, two]), odd


def band_table():
    near = ORDER[:CLASS] // FOLD
    apart = FOLD * (near[:, None] - near[None, :])
    blocks = [np.abs(apart + shift) <= HW for shift in (0, -1, 1)]
    return np.concatenate(blocks, axis=0).astype(ml_dtypes.bfloat16)


def inverse_tables():
    freqs = K0 + ORDER.astype(np.int64)
    delays = (np.arange(2 * LAGQ, dtype=np.int64) - NLAG // 2) * DEC
    phase = np.mod(freqs[:, None] * delays[None, :], NT)
    angle = phase.astype(np.float64) * (2.0 * math.pi / NT)
    scale = 1.0 / math.sqrt(NB)
    real = (np.cos(angle) * scale).reshape(SLICES, 1, LANES, 2 * LAGQ)
    imag = (-np.sin(angle) * scale).reshape(SLICES, 1, LANES, 2 * LAGQ)
    rows = np.concatenate([real, imag], axis=1).reshape(FOLD, 2 * CLASS, 2 * LAGQ)
    zero = rows[0][:, :LAGQ]
    two = rows[2][:, :LAGQ]
    odd = np.concatenate([rows[1], rows[3]], axis=0)
    return [table.astype(np.float32).astype(ml_dtypes.bfloat16) for table in (zero, two, odd)]


def two_terms(values):
    high = values.astype(jnp.bfloat16)
    low = (values - high.astype(jnp.float32)).astype(jnp.bfloat16)
    return high, low


def two_term_dot(values_ref, table):
    rows = values_ref.shape[0] // 2
    both = jnp.dot(values_ref[...], table, preferred_element_type=jnp.float32)
    return both[:rows] + both[rows:]


def ranks(mask_row):
    shape = (LANES, LANES)
    upto = lax.broadcasted_iota(jnp.int32, shape, 0) <= lax.broadcasted_iota(jnp.int32, shape, 1)
    row = jnp.broadcast_to(mask_row, (META, LANES)).astype(jnp.bfloat16)
    count = jnp.dot(row, upto.astype(jnp.float32).astype(jnp.bfloat16), preferred_element_type=jnp.float32)
    return jnp.where(mask_row > 0, count[0:1] - 1.0, -1.0)


def sorted_rows(mask_row):
    rank = ranks(mask_row)
    rows = []
    for seg in range(2):
        row, below, done = jnp.full_like(rank, -1.0), 0, 0
        for tier in TIERS:
            inside = (rank >= below) & (rank < below + tier)
            row = jnp.where(inside, rank - below + done + seg * tier, row)
            below, done = below + tier, done + 2 * tier
        rows.append(row)
    rows = jnp.concatenate(rows, axis=1)
    return rows == lax.broadcasted_iota(jnp.int32, (PAIR, PAIR), 0).astype(jnp.float32)


def place_order():
    place = lax.broadcasted_iota(jnp.int32, (PAIR, PAIR), 0)
    row = lax.broadcasted_iota(jnp.int32, (PAIR, PAIR), 1)
    inside = place % LANES
    return (place // LANES) * LANES + (inside % G) * (LANES // G) + inside // G == row


def spectra_kernel(relative, with_meta, kept, skip, alone, *refs):
    f32, bf16 = jnp.float32, jnp.bfloat16
    refs = list(refs)
    here_ref = refs.pop(0) if relative else None
    x_any, mask_ref, owner_ref, bins_ref, even_any, odd_any, band_any = refs[:7]
    x_refs, even_ref, odd_ref, band_ref, x_came, arrived, plus, minus, v, ab, early, others, windows = refs[-13:]
    out_refs = refs[7:-14] if relative else refs[7:-13]
    head = refs[-14] if relative else out_refs[0]
    spares = out_refs[1 - len(TIERS):] if kept < PAIR else []
    step, steps = pl.program_id(0), pl.num_programs(0)
    first = step == 0
    rows = x_refs.shape[1]
    slot = 0 if alone else lax.rem(step, 2)
    at_first = (lambda act: act()) if alone else pl.when(first)
    moves = ((even_any, even_ref), (odd_any, odd_ref), (band_any, band_ref))
    copies = [pltpu.make_async_copy(source, into, arrived.at[i]) for i, (source, into) in enumerate(moves)]

    def trace_copy(block, slot):
        at = pl.ds(pl.multiple_of(block * rows + skip, LANES), rows)
        return pltpu.make_async_copy(x_any.at[at], x_refs.at[slot], x_came.at[slot])

    @at_first
    def start():
        trace_copy(0, 0).start()
        for copy in copies:
            copy.start()

    mask = mask_ref[...].astype(f32)
    if kept < PAIR:
        chosen = sorted_rows(mask)
    else:
        chosen = place_order() & (jnp.concatenate([mask, mask], axis=1) > 0)
    chosen = chosen.astype(f32).astype(bf16)

    trace_copy(step, slot).wait()

    if not alone:

        @pl.when(step + 1 < steps)
        def ahead():
            trace_copy(step + 1, 1 - slot).start()

    @at_first
    def table_waits():
        for copy in copies:
            copy.wait()

    x_ref = x_refs.at[slot]
    x = [x_ref[:, m * QUARTER:(m + 1) * QUARTER].astype(f32) for m in range(FOLD)]
    even, odd = x[0] + x[2], x[1] + x[3]
    u = even + odd
    plus[:rows], plus[rows:] = two_terms(u[:, :EIGHTH] + u[:, EIGHTH:])
    minus[:rows], minus[rows:] = two_terms(u[:, :EIGHTH] - u[:, EIGHTH:])
    u = even - odd
    v[:rows], v[rows:2 * rows] = two_terms(u[:, :EIGHTH])
    v[2 * rows:3 * rows], v[3 * rows:] = two_terms(u[:, EIGHTH:])
    ab[:rows], ab[rows:2 * rows] = two_terms(x[0] - x[2])
    ab[2 * rows:3 * rows], ab[3 * rows:] = two_terms(x[1] - x[3])

    for half, ref in enumerate((plus, minus)):
        both = two_term_dot(ref, even_ref[0, :, half * PAIR:(half + 1) * PAIR])
        early[:, half * LANES:(half + 1) * LANES] = both[:, :LANES]
        early[:, CLASS + half * LANES:CLASS + (half + 1) * LANES] = both[:, LANES:]
    turned = jnp.dot(v[...], even_ref[1], preferred_element_type=f32)
    straight = turned[:rows] + turned[rows:2 * rows]
    turned = turned[2 * rows:3 * rows] + turned[3 * rows:]
    lanes = [slice(i * LANES, (i + 1) * LANES) for i in range(4)]
    early[:, 2 * CLASS:2 * CLASS + LANES] = straight[:, lanes[0]] + turned[:, lanes[2]]
    early[:, 2 * CLASS + LANES:3 * CLASS] = straight[:, lanes[1]] - turned[:, lanes[3]]
    early[:, 3 * CLASS:3 * CLASS + LANES] = straight[:, lanes[2]] - turned[:, lanes[0]]
    early[:, 3 * CLASS + LANES:] = straight[:, lanes[3]] + turned[:, lanes[1]]
    turned = jnp.dot(ab[...], odd_ref[...], preferred_element_type=f32)
    straight = turned[:rows] + turned[rows:2 * rows]
    turned = turned[2 * rows:3 * rows] + turned[3 * rows:]
    columns = [slice(i * CLASS, (i + 1) * CLASS) for i in range(4)]
    others[:, columns[0]] = straight[:, columns[0]] + turned[:, columns[1]]
    others[:, columns[1]] = straight[:, columns[1]] - turned[:, columns[0]]
    others[:, columns[2]] = straight[:, columns[2]] - turned[:, columns[3]]
    others[:, columns[3]] = straight[:, columns[3]] + turned[:, columns[2]]

    holders = [(early, 0), (others, 0), (early, 2 * CLASS), (others, 2 * CLASS)]
    power = []
    for ref, start in holders:
        real, imag = ref[:, start:start + CLASS], ref[:, start + CLASS:start + 2 * CLASS]
        power.append(real * real + imag * imag)
    before = [jnp.zeros_like(power[0]), power[0], power[0] + power[1], power[0] + power[1] + power[2]]
    after = [power[1] + power[2] + power[3], power[2] + power[3], power[3], jnp.zeros_like(power[0])]
    for which in range(FOLD):
        at = slice(which * rows, (which + 1) * rows)
        windows[at, :CLASS] = power[which].astype(bf16)
        windows[at, CLASS:2 * CLASS] = before[which].astype(bf16)
        windows[at, 2 * CLASS:] = after[which].astype(bf16)
    sums = jnp.dot(windows[...], band_ref[...], preferred_element_type=f32)
    weight = []
    for which in range(FOLD):
        lane = lax.broadcasted_iota(jnp.int32, (1, CLASS), 1)
        bin_ = ((lane % LANES) * 2 + lane // LANES) * FOLD + which
        within = jnp.minimum(bin_ + HW, NB - 1) - jnp.maximum(bin_ - HW, 0) + 1
        mean = sums[which * rows:(which + 1) * rows] * (1.0 / within.astype(f32))
        weight.append(lax.rsqrt(mean + EPSILON))
    for piece in range(SLICES):
        ref, column = holders[piece // 2]
        column += (piece % 2) * LANES
        scale = weight[piece // 2][:, (piece % 2) * LANES:(piece % 2 + 1) * LANES]
        real = (ref[:, column:column + LANES] * scale).astype(bf16)
        imag = (ref[:, CLASS + column:CLASS + column + LANES] * scale).astype(bf16)
        both = jnp.concatenate([real, imag], axis=1)
        for pair in range(rows // PAIR):
            sorted_ = jnp.dot(chosen, both[pair * PAIR:(pair + 1) * PAIR], preferred_element_type=f32).astype(bf16)
            head[piece, pair * kept:(pair + 1) * kept, :] = sorted_[:kept]
            start = kept
            for spare, tier in zip(spares, TIERS[1:]):
                spare[piece, pair * 2 * tier:(pair + 1) * 2 * tier, :] = sorted_[start:start + 2 * tier]
                start += 2 * tier
    if with_meta:
        tiles = owner_ref.shape[1]
        labels = (owner_ref[...] * BIN_DEV + bins_ref[...]).astype(f32)
        for piece in range(SLICES):
            at = pl.ds(rows // PAIR * kept, META)
            head[piece, at, :] = jnp.zeros((META, 2 * LANES), bf16)
            head[piece, at, :LANES] = jnp.broadcast_to(mask, (META, LANES)).astype(bf16)
            head[piece, at, LANES:LANES + tiles] = jnp.broadcast_to(labels, (META, tiles)).astype(bf16)
    if relative:
        for other in range(SLICES):
            out_refs[other][...] = head[lax.rem(here_ref[0] + other, SLICES)]


def spectra(traces, mask, owners, bins, first_row, rows, block, kept, here=None, with_meta=False):
    relative = here is not None
    tables = [jnp.asarray(table) for table in forward_tables() + (band_table(),)]
    whole = lambda array: pl.BlockSpec(array.shape, lambda i, *_: (0, 0))
    in_place = pl.BlockSpec(memory_space=pl.ANY)
    f32, bf16 = jnp.float32, jnp.bfloat16
    pairs = block // PAIR
    scratch = [
        pltpu.VMEM((2, block, NT), bf16),
    ] + [pltpu.VMEM(table.shape, bf16) for table in tables] + [
        pltpu.SemaphoreType.DMA((2,)),
        pltpu.SemaphoreType.DMA((3,)),
    ]
    scratch += [pltpu.VMEM((terms * block, EIGHTH), bf16) for terms in (2, 2, 4)]
    scratch += [pltpu.VMEM((4 * block, QUARTER), bf16)]
    scratch += [pltpu.VMEM((block, 4 * CLASS), f32)] * 2
    scratch += [pltpu.VMEM((FOLD * block, 3 * CLASS), bf16)]
    if relative:
        scratch = [pltpu.VMEM((SLICES, pairs * kept, 2 * LANES), bf16)] + scratch
        out_specs = [pl.BlockSpec((pairs * kept, 2 * LANES), lambda i, *_: (i, 0))] * SLICES
        out_shape = [jax.ShapeDtypeStruct((rows // PAIR * kept, 2 * LANES), bf16)] * SLICES
    else:
        extra = META if with_meta else 0
        out_specs = [pl.BlockSpec((SLICES, pairs * kept + extra, 2 * LANES), lambda i, *_: (0, i, 0))]
        out_shape = [jax.ShapeDtypeStruct((SLICES, rows // PAIR * kept + extra, 2 * LANES), bf16)]
    for tier in TIERS[1:] if kept < PAIR else ():
        out_specs.append(pl.BlockSpec((SLICES, pairs * 2 * tier, 2 * LANES), lambda i, *_: (0, i, 0)))
        out_shape.append(jax.ShapeDtypeStruct((SLICES, rows // LANES * tier, 2 * LANES), bf16))
    return pl.pallas_call(
        functools.partial(spectra_kernel, relative, with_meta, kept, first_row, rows == block),
        grid_spec=pltpu.PrefetchScalarGridSpec(
            num_scalar_prefetch=1 if relative else 0,
            grid=(rows // block,),
            in_specs=[in_place, whole(mask), whole(owners), whole(bins)] + [in_place] * len(tables),
            out_specs=out_specs,
            scratch_shapes=scratch,
        ),
        out_shape=out_shape,
        compiler_params=pltpu.CompilerParams(vmem_limit_bytes=VMEM),
        cost_estimate=pl.CostEstimate(
            flops=14 * rows * NB * NB, bytes_accessed=rows * NT * 3 + 8 * NB * NB, transcendentals=rows * NB
        ),
        name="spectra",
    )(*([here] if relative else []), traces, mask, owners, bins, *tables)


def pair_sums(block_refs, pairs, steps, tiles):
    f32 = jnp.float32
    done = 0
    groups, current = [], []
    for pair in pairs:
        members = {m for p in current + [pair] for m in p}
        if current and 4 * (len(current) + 1) + 4 * len(members) > 60:
            groups.append(current)
            current = []
        current = current + [pair]
    groups.append(current)
    for group in groups:
        needed = sorted({m for pair in group for m in pair})

        def body(step, sums):
            at = pl.ds(pl.multiple_of(step * G, G), G)
            real = {m: block_refs[m][at, :LANES].astype(f32) for m in needed}
            imag = {m: block_refs[m][at, LANES:].astype(f32) for m in needed}
            new = []
            for (p, q), (re, im) in zip(group, sums):
                re = re + (real[p] * real[q] + imag[p] * imag[q])
                im = im + (imag[p] * real[q] - real[p] * imag[q])
                new.append((re, im))
            return tuple(new)

        zero = jnp.zeros((G, LANES), f32)
        sums = lax.fori_loop(0, steps, body, tuple((zero, zero) for _ in group), unroll=2)
        for re, im in sums:
            tiles[done:done + G, :LANES] = re
            tiles[done:done + G, LANES:] = im
            done += G


def place_rows(head_ref, spare_refs, first_pair, places, out_ref):
    for pair in range(out_ref.shape[0] // PAIR):
        rows = [head_ref[pair * KEPT:(pair + 1) * KEPT]]
        for spare_ref, tier in zip(spare_refs, TIERS[1:]):
            at = (first_pair + pair) * 2 * tier
            rows.append(spare_ref[at:at + 2 * tier])
        placed = jnp.dot(places, jnp.concatenate(rows, axis=0), preferred_element_type=jnp.float32)
        out_ref[pair * PAIR:(pair + 1) * PAIR, :] = placed.astype(out_ref.dtype)


def cross_kernel(plan, here_ref, *refs):
    f32 = jnp.float32
    refs = list(refs)
    take = lambda count: [refs.pop(0) for _ in range(count)]
    ready, heads = take(plan["ready"]), take(plan["heads"])
    *spare_refs, places_ref = take(len(TIERS)) if heads else [None]
    (rows_ref,) = take(1)
    before_ref = refs.pop(0) if plan["before"] else None
    out_ref = refs.pop(0)
    placed = take(len(plan["slots"])) if plan["hand_on"] else None
    tiles = refs.pop(0)
    if plan["stacked"]:
        source = heads[0] if heads else ready[0]
        count = source.shape[0]
        heads = [source.at[m] for m in range(count)] if heads else []
        ready = [] if heads else [source.at[m] for m in range(count)]
    if heads:
        if placed is None:
            (room,) = refs
            placed = [room.at[i] for i in range(len(heads))]
        for i, head in enumerate(heads):
            block = i if plan["stacked"] else lax.rem(here_ref[0] - plan["slots"][i] + SLICES, SLICES)
            spares = [spare_ref.at[block] for spare_ref in spare_refs]
            place_rows(head, spares, plan["first_pair"], places_ref[block], placed[i])
        ready = ready + placed
    pair_sums(ready, plan["pairs"], plan["steps"], tiles)
    bins, count = out_ref.shape[-2], tiles.shape[0]
    wanted = rows_ref[0:1, :] == lax.broadcasted_iota(jnp.int32, (bins, count), 0).astype(f32)
    high, low = two_terms(tiles[...])
    stacked = []
    for half in range(2):
        weights = jnp.where(wanted, jnp.broadcast_to(rows_ref[half + 1:half + 2, :], (bins, count)), 0.0)
        weights = jnp.concatenate(two_terms(weights), axis=0)
        at = slice(half * LANES, (half + 1) * LANES)
        both = jnp.dot(weights, high[:, at], preferred_element_type=f32)
        both = both[:bins] + both[bins:]
        stacked.append(both + jnp.dot(weights[:bins], low[:, at], preferred_element_type=f32))
    stacked = jnp.concatenate(stacked, axis=1)
    if before_ref is not None:
        stacked += before_ref[...]
    if len(out_ref.shape) == 2:
        out_ref[...] = stacked
    else:
        for copy in range(out_ref.shape[0]):
            out_ref[copy] = stacked.astype(out_ref.dtype)


def cross(here, pairs, steps, bins, weights, ready=(), heads=(), slots=(), spares=(), first_pair=0, places=None,
          before=None, copies=None, hand_on=False, stacked=False):
    shape = (bins, 2 * LANES)
    inputs = list(ready) + list(heads) + (list(spares) + [places] if heads else []) + [weights]
    if before is not None:
        inputs.append(before)
    if copies is None:
        out_shape = [jax.ShapeDtypeStruct(shape, jnp.float32)]
    else:
        out_shape = [jax.ShapeDtypeStruct((copies,) + shape, jnp.bfloat16)]
    scratch = [pltpu.VMEM((len(pairs) * G, 2 * LANES), jnp.float32)]
    if hand_on:
        out_shape += [jax.ShapeDtypeStruct((G * steps, 2 * LANES), jnp.bfloat16)] * len(heads)
    elif heads:
        count = heads[0].shape[0] if stacked else len(heads)
        scratch.append(pltpu.VMEM((count, G * steps, 2 * LANES), jnp.bfloat16))
    plan = dict(
        ready=len(ready), heads=len(heads), slots=slots, before=before is not None, hand_on=hand_on,
        stacked=stacked, first_pair=first_pair, pairs=pairs, steps=steps,
    )
    result = pl.pallas_call(
        functools.partial(cross_kernel, plan),
        in_specs=[pl.BlockSpec(memory_space=pltpu.SMEM)] + [pl.BlockSpec(memory_space=pltpu.VMEM)] * len(inputs),
        out_shape=out_shape,
        scratch_shapes=scratch,
        compiler_params=pltpu.CompilerParams(vmem_limit_bytes=VMEM if stacked and copies else VMEM_SMALL),
        cost_estimate=pl.CostEstimate(
            flops=8 * G * steps * LANES * len(pairs), bytes_accessed=4 * G * steps * LANES * len(pairs), transcendentals=0
        ),
        name="cross",
    )(here, *inputs)
    return result if hand_on else result[0]


def weights_kernel(blocks, total_segs, here_ref, meta_ref, *refs):
    f32, bf16 = jnp.float32, jnp.bfloat16
    meta = jnp.concatenate([meta_ref[b, 0:1, :] for b in range(blocks)], axis=0)
    masks, labels = meta[:, :LANES], meta[:, LANES:]
    empty = jnp.zeros((R, LANES), bf16)
    padded = jnp.concatenate([masks.astype(f32), empty.astype(f32)], axis=0)
    half = len(refs) // 2
    places_ref = refs[-1]
    in_place = place_order().astype(f32).astype(bf16)
    for b in range(blocks):
        rows = sorted_rows(masks[b:b + 1].astype(f32)).astype(f32).astype(bf16)
        places = lax.dot_general(in_place, rows, (((1,), (1,)), ((), ())), preferred_element_type=f32)
        places_ref[b] = places.astype(bf16)
    for ends_ref, out_ref in zip(refs[:half], refs[half:-1]):
        lanes = out_ref.shape[1]
        first, second = ends_ref[0:1, :], ends_ref[1:2, :]
        slots = first < 0
        held = [jnp.where(slots, lax.rem(here_ref[0] + end + 2 * blocks, blocks), end) for end in (first, second)]
        low, far = jnp.minimum(held[0], held[1]), jnp.abs(held[0] - held[1])
        sign = jnp.where(held[0] < held[1], 1.0, -1.0)
        block = lax.broadcasted_iota(jnp.int32, (blocks, lanes), 0)
        group = lax.broadcasted_iota(jnp.int32, (LANES, lanes), 1) % G
        place = lax.broadcasted_iota(jnp.int32, (LANES, lanes), 0)
        chosen = (place == (far - 1) * G + group).astype(f32).astype(bf16)
        label = jnp.dot(labels, chosen, preferred_element_type=f32)
        label = jnp.sum(jnp.where(block == low, label, 0.0), axis=0, keepdims=True)
        member = (place // (LANES // G) == group).astype(f32).astype(bf16)
        count = jnp.zeros((1, lanes), f32)
        for d in range(1, R + 1):
            both = (padded[:blocks] * padded[d:d + blocks]).astype(bf16)
            of_block = jnp.dot(both, member, preferred_element_type=f32)
            count += jnp.sum(jnp.where((block == low) & (far == d), of_block, 0.0), axis=0, keepdims=True)
        scale = jnp.where(far <= R, 1.0 / (total_segs * jnp.maximum(count, 1.0)), 0.0)
        out_ref[...] = jnp.concatenate([label, scale, scale * sign, jnp.zeros((5, lanes), f32)], axis=0)


def pair_weights(here, meta, at, total_segs, pair_lists):
    blocks = meta.shape[0]
    ends = [jnp.asarray(np.repeat(np.array(pairs, np.int32).T, G, axis=1)) for pairs in pair_lists]
    whole = lambda shape: pl.BlockSpec(shape, lambda i, *_: (0, 0))
    shapes = [(8, G * len(pairs)) for pairs in pair_lists]
    return pl.pallas_call(
        functools.partial(weights_kernel, blocks, total_segs),
        grid_spec=pltpu.PrefetchScalarGridSpec(
            num_scalar_prefetch=1,
            grid=(1,),
            in_specs=[pl.BlockSpec((blocks, META, 2 * LANES), lambda i, *_: (0, at // META, 0))]
            + [whole(end.shape) for end in ends],
            out_specs=[whole(shape) for shape in shapes]
            + [pl.BlockSpec((blocks, PAIR, PAIR), lambda i, *_: (0, 0, 0))],
        ),
        out_shape=[jax.ShapeDtypeStruct(shape, jnp.float32) for shape in shapes]
        + [jax.ShapeDtypeStruct((blocks, PAIR, PAIR), jnp.bfloat16)],
        compiler_params=pltpu.CompilerParams(vmem_limit_bytes=VMEM_SMALL),
        name="weights",
    )(here, meta, *ends)


def lags_kernel(stacks_ref, zero_ref, two_ref, odd_ref, out_ref):
    f32 = jnp.float32
    copies = stacks_ref.shape[0] // SLICES
    pieces = []
    for piece in range(SLICES):
        total = stacks_ref[piece].astype(f32)
        for copy in range(1, copies):
            total += stacks_ref[copy * SLICES + piece].astype(f32)
        pieces.append(total)

    def product(values, table):
        both = jnp.dot(jnp.concatenate(two_terms(values), axis=0), table, preferred_element_type=f32)
        return both[:BIN_DEV] + both[BIN_DEV:]

    zero = product(jnp.concatenate(pieces[0:2], axis=1), zero_ref[...])
    two = product(jnp.concatenate(pieces[4:6], axis=1), two_ref[...])
    odd = product(jnp.concatenate(pieces[2:4] + pieces[6:8], axis=1), odd_ref[...])
    plus, minus = zero + two, zero - two
    out_ref[:, :LAGQ] = plus + odd[:, :LAGQ]
    out_ref[:, LAGQ:2 * LAGQ] = minus + odd[:, LAGQ:]
    out_ref[:, 2 * LAGQ:3 * LAGQ] = plus - odd[:, :LAGQ]
    out_ref[:, 3 * LAGQ:] = minus - odd[:, LAGQ:]


def lags(stacks):
    tables = [jnp.asarray(table) for table in inverse_tables()]
    return pl.pallas_call(
        lags_kernel,
        out_shape=jax.ShapeDtypeStruct((BIN_DEV, NLAG), jnp.float32),
        compiler_params=pltpu.CompilerParams(vmem_limit_bytes=VMEM_SMALL),
        name="lags",
    )(stacks, *tables)


def fixed_pairs(blocks):
    return [(b, b + d) for b in range(blocks) for d in range(1, R + 1) if b + d < blocks]


def sent_along(x, mask, owners, bins, total_segs):
    seg_count = lax.axis_size("seg")
    count = lax.axis_size("chan")
    early = EARLY_SEGS * LANES
    late = x.shape[0] - early
    here = lax.axis_index("chan").astype(jnp.int32).reshape(1)
    first, *spare_early = spectra(x, mask, owners, bins, 0, early, early, KEPT, with_meta=True)
    first = lax.all_to_all(first, "chan", split_axis=0, concat_axis=0, tiled=True)
    second = list(spectra(x, mask, owners, bins, early, late, PAIR, KEPT, here=here))
    spare_late = second[SLICES:]
    at = early // PAIR * KEPT
    most = jnp.max(jnp.sum(first[:, at, :LANES].astype(jnp.float32), axis=1))
    spares, below = [], TIERS[0]
    for tier, *parts in zip(TIERS[1:], spare_early, spare_late):
        spares.append(lax.cond(
            most > below,
            lambda parts: lax.all_to_all(jnp.concatenate(parts, axis=1), "chan", split_axis=0, concat_axis=0, tiled=True),
            lambda parts: jnp.zeros((count, sum(part.shape[1] for part in parts), 2 * LANES), jnp.bfloat16),
            parts,
        ))
        below += tier

    *late_sent, _ = lax.optimization_barrier((second[SENT[-2]], second[SENT[-1]], tuple(spares)))
    second[SENT[-2]], second[SENT[-1]] = late_sent
    slots = {0: second[0]}
    for shift in SENT:
        slots[shift] = lax.ppermute(second[shift], "chan", [(i, (i + shift) % count) for i in range(count)])

    fixed = fixed_pairs(count)
    known = (0,) + SENT
    stages = [
        [(i, j) for j in range(start, end) for i in range(j)] for start, end in zip((1,) + STAGES, STAGES)
    ]
    as_slots = lambda pairs: [(-known[i] - count, -known[j] - count) for i, j in pairs]
    weights = pair_weights(here, first, at, total_segs, [fixed] + [as_slots(pairs) for pairs in stages])
    places = weights[-1]
    bins = count * BIN_DEV
    stacks = cross(
        here, fixed, early // G, bins, weights[0], heads=[first], spares=spares, places=places, stacked=True
    )
    ready, start = [], 0
    for end, pairs, weight in zip(STAGES, stages, weights[1:]):
        final = end == len(known)
        result = cross(
            here, pairs, late // G, bins, weight,
            ready=ready, heads=[slots[slot] for slot in known[start:end]], slots=known[start:end],
            spares=spares, first_pair=early // PAIR, places=places, before=stacks,
            copies=seg_count if final else None, hand_on=not final,
        )
        if final:
            return result
        stacks, ready, start = result[0], ready + list(result[1:]), end


def sent_at_once(x, mask, owners, bins, total_segs):
    seg_count = lax.axis_size("seg")
    count = lax.axis_size("chan")
    rows, chans = x.shape[0], mask.shape[1]
    narrow = NB // count
    splits = LANES // narrow
    here = lax.axis_index("chan").astype(jnp.int32).reshape(1)
    own = jnp.concatenate([mask, owners * BIN_DEV + bins], axis=1)
    every = lax.all_gather(own, "chan", axis=0, tiled=True).astype(jnp.bfloat16)
    every = jnp.pad(every, ((0, 0), (0, 2 * LANES - every.shape[1])))
    every = jnp.broadcast_to(every[:, None, :], (count, META, 2 * LANES))
    fixed = fixed_pairs(count)
    weights = pair_weights(here, every, 0, total_segs, [fixed])[:1]
    (outgoing,) = spectra(x, mask, owners, bins, 0, rows, PAIR, PAIR)
    outgoing = outgoing.reshape(SLICES, rows, 2, splits, narrow).transpose(0, 3, 1, 2, 4)
    outgoing = outgoing.reshape(count, rows, 2 * narrow)
    wide = lax.all_to_all(outgoing, "chan", split_axis=0, concat_axis=0, tiled=True)
    wide = jnp.pad(wide.reshape(count, rows, 2, narrow), ((0, 0), (0, 0), (0, 0), (0, LANES - narrow)))
    wide = wide.reshape(count, rows, 2 * LANES)
    stacks = cross(
        here, fixed, rows // G, count * BIN_DEV, weights[0], ready=[wide], copies=seg_count, stacked=True
    )
    return stacks.reshape(-1, 2, LANES)[..., :narrow]


def per_device(traces, channel_mask, owner_ids, local_bins):
    seg_count = lax.axis_size("seg")
    count = lax.axis_size("chan")
    segs, chans, length = traces.shape
    x = traces.reshape(segs * chans, length)
    mask = channel_mask.reshape(1, chans)
    owners = owner_ids.reshape(1, -1)
    if count == SLICES:
        stacks = sent_along(x, mask, owners, local_bins, segs * seg_count)
        stacks = stacks.reshape(seg_count * count, BIN_DEV, 2 * LANES)
        stacks = lax.all_to_all(stacks, ("seg", "chan"), split_axis=0, concat_axis=0, tiled=True)
    else:
        narrow = NB // count
        stacks = sent_at_once(x, mask, owners, local_bins, segs * seg_count)
        stacks = stacks.reshape(seg_count * count, BIN_DEV, 2 * narrow)
        stacks = lax.all_to_all(stacks, ("seg", "chan"), split_axis=0, concat_axis=0, tiled=True)
        stacks = stacks.reshape(seg_count, SLICES, count // SLICES, BIN_DEV, 2, narrow)
        stacks = stacks.transpose(0, 1, 3, 4, 2, 5).reshape(seg_count * SLICES, BIN_DEV, 2 * LANES)
    return lags(stacks)


def solution(mesh):
    in_specs = (P("seg", "chan", None), P("chan"), P("chan", None, None), P("chan", None))
    out_specs = P("chan", None)
    return jax.shard_map(
        per_device, mesh=mesh, in_specs=in_specs, out_specs=out_specs, check_vma=False
    )
```

profile of v0, /device:TPU:0, one launch (start us, length us, event | category | flops | bytes accessed | tf_op | source)
XLA Modules:
  0.0 110.0 jit_solution(14983906630338713890)
XLA Ops:
  0.0 9.0 %spectra.3 = (bf16[8,224,256]{2,1,0:T(8,128)(2,1)}, bf16[8,16,256]{2,1,0:T(8,128)(2,1)S(1)}, bf16[8,32,256]{2,1,0:T(8,128)(2,1)S(1)}) custom-call(bf16[1024,4096]{1,0:T(8,128)(2,1)} %bitcast.6, s32[1,128]{1,0:T(1,128)} %bitcast.8, s32[1,64]{1,0:T(1,128)} %bitcast.10, s32[1,64]{1,0:T(1,128)} %refs_3_.1, bf16[2,512,512]{2,1,0:T(8,128)(2,1)} %constant.34.clone.refs_5_.refs_4_, ...), custom_call_target="tpu_custom_call" | custom-call | flops 3758096384 | bytes 11534336 | tf_op jit(solution)/shard_map/spectra/pallas_call | solution.py:282
  9.0 7.3 %all-to-all-start.2 = ((bf16[8,224,256]{2,1,0:T(8,128)(2,1)}), bf16[8,224,256]{2,1,0:T(8,128)(2,1)S(1)}, u32[]{:S(2)}, u32[]{:S(2)}) async-start(bf16[8,224,256]{2,1,0:T(8,128)(2,1)} %get-tuple-element.55), calls=%async_computation.2 | async-start | bytes 1835008 | tf_op jit(solution)/shard_map/all_to_all | solution.py:527
  16.3 19.1 %spectra.2 = (bf16[624,256]{1,0:T(8,128)(2,1)}, bf16[624,256]{1,0:T(8,128)(2,1)}, bf16[624,256]{1,0:T(8,128)(2,1)}, bf16[624,256]{1,0:T(8,128)(2,1)}, bf16[624,2...) custom-call(s32[1]{0:T(128)} %bitcast.refs_0_.here_ref, ...), custom_call_target="tpu_custom_call" | custom-call | flops 11274289152 | bytes 17825792 | tf_op jit(solution)/shard_map/spectra/pallas_call | solution.py:282
  35.4 0.0 copy-start.4
  35.4 0.0 copy-start.5
  35.4 0.0 copy-start.6
  35.4 2.9 %collective-permute-start = (bf16[624,256]{1,0:T(8,128)(2,1)}, bf16[624,256]{1,0:T(8,128)(2,1)S(1)}, u32[]{:S(2)}, u32[]{:S(2)}) collective-permute-start(bf16[624,256]{1,0:T(8,128)(2,1)} %get-tuple-element.50), channel_id=1, source_target_pairs={{0,4},{1,5},{2,6},{3,7},{4,0},{5,1},{6,2},{7,3},{8,12},{9,13},{10,... | collective-permute-start | bytes 958472 | tf_op jit(solution)/shard_map/ppermute | solution.py:546
  38.4 1.5 %collective-permute-start.1 = (bf16[624,256]{1,0:T(8,128)(2,1)}, bf16[624,256]{1,0:T(8,128)(2,1)S(1)}, u32[]{:S(2)}, u32[]{:S(2)}) collective-permute-start(bf16[624,256]{1,0:T(8,128)(2,1)} %get-tuple-element.51), channel_id=1, source_target_pairs={{0,1},{1,2},{2,3},{3,4},{4,5},{5,6},{6,7},{7,0},{8,9},{9,10},{10,1... | collective-permute-start | bytes 958472 | tf_op jit(solution)/shard_map/ppermute | solution.py:546
  39.8 3.2 %collective-permute-start.2 = (bf16[624,256]{1,0:T(8,128)(2,1)}, bf16[624,256]{1,0:T(8,128)(2,1)S(1)}, u32[]{:S(2)}, u32[]{:S(2)}) collective-permute-start(bf16[624,256]{1,0:T(8,128)(2,1)} %get-tuple-element.52), channel_id=1, source_target_pairs={{0,7},{1,0},{2,1},{3,2},{4,3},{5,4},{6,5},{7,6},{8,15},{9,8},{10,9... | collective-permute-start | bytes 958472 | tf_op jit(solution)/shard_map/ppermute | solution.py:546
  43.1 3.8 %collective-permute-start.4 = (bf16[624,256]{1,0:T(8,128)(2,1)}, bf16[624,256]{1,0:T(8,128)(2,1)S(1)}, u32[]{:S(2)}, u32[]{:S(2)}) collective-permute-start(bf16[624,256]{1,0:T(8,128)(2,1)} %get-tuple-element.54), channel_id=1, source_target_pairs={{0,5},{1,6},{2,7},{3,0},{4,1},{5,2},{6,3},{7,4},{8,13},{9,14},{10,... | collective-permute-start | bytes 958472 | tf_op jit(solution)/shard_map/ppermute | solution.py:546
  46.9 0.1 fusion
  47.1 0.6 reduce_max.9
  48.9 0.7 copy-done.7
  49.6 21.3 %collective-permute-done.refs_1_ = bf16[624,256]{1,0:T(8,128)(2,1)S(1)} collective-permute-done((bf16[624,256]{1,0:T(8,128)(2,1)}, bf16[624,256]{1,0:T(8,128)(2,1)S(1)}, u32[]{:S(2)}, u32[]{:S(2)}) %collective-permute-start) | collective-permute-done | bytes 319520 | tf_op jit(solution)/shard_map/ppermute | solution.py:546
  70.9 3.8 %collective-permute-start.6 = (bf16[624,256]{1,0:T(8,128)(2,1)}, bf16[624,256]{1,0:T(8,128)(2,1)S(1)}, u32[]{:S(2)}, u32[]{:S(2)}) collective-permute-start(bf16[624,256]{1,0:T(8,128)(2,1)} %get-tuple-element.72), channel_id=1, source_target_pairs={{0,6},{1,7},{2,0},{3,1},{4,2},{5,3},{6,4},{7,5},{8,14},{9,15},{10,... | collective-permute-start | bytes 958472 | tf_op jit(solution)/shard_map/ppermute | solution.py:546
  74.7 1.3 %weights.1 = (f32[8,352]{1,0:T(8,128)S(1)}, f32[8,240]{1,0:T(8,128)S(1)}, f32[8,208]{1,0:T(8,128)S(1)}, bf16[8,256,256]{2,1,0:T(8,128)(2,1)S(1)}) custom-call(s32[1]{0:T(128)} %bitcast.refs_0_.here_ref, bf16[8,224,256]{2,1,0:T(8,128)(2,1)S(1)} %all-to-all-done.2.meta_ref.refs_0_, s32[2,352]{1,0:T(2,128)S(1)} %copy-done.4, s32[2,240]{1,0:T(2,128)S(1)} %copy-done.6, ...), custom_call_target="tpu_custom_call" | custom-call | tf_op jit(solution)/shard_map/weights/pallas_call | solution.py:465
  76.1 2.7 %cross.3.refs_10_ = f32[64,256]{1,0:T(8,128)S(1)} custom-call(s32[1]{0:T(128)} %bitcast.refs_0_.here_ref, bf16[8,224,256]{2,1,0:T(8,128)(2,1)S(1)} %all-to-all-done.2.meta_ref.refs_0_, bf16[8,64,256]{2,1,0:T(8,128)(2,1)} %copy-done.7, bf16[8,128,256]{2,1,0:T(8,128)(2,1)S(1)} %get-tuple-element.76.refs_2_.refs_7_.refs_9_, ...), custom_call_target="tpu_custom_call" | custom-call | flops 5767168 | bytes 2883584 | tf_op jit(solution)/shard_map/cross/pallas_call | solution.py:410
  78.8 3.3 %collective-permute-done.3.refs_4_ = bf16[624,256]{1,0:T(8,128)(2,1)S(1)} collective-permute-done((bf16[624,256]{1,0:T(8,128)(2,1)}, bf16[624,256]{1,0:T(8,128)(2,1)S(1)}, u32[]{:S(2)}, u32[]{:S(2)}) %collective-permute-start.3) | collective-permute-done | bytes 319520 | tf_op jit(solution)/shard_map/ppermute | solution.py:546
  82.1 3.2 %cross.4 = (f32[64,256]{1,0:T(8,128)S(1)}, bf16[768,256]{1,0:T(8,128)(2,1)S(1)}, bf16[768,256]{1,0:T(8,128)(2,1)S(1)}, bf16[768,256]{1,0:T(8,128)(2,1)S(1)}, bf1...) custom-call(s32[1]{0:T(128)} %bitcast.refs_0_.here_ref, ...), custom_call_target="tpu_custom_call" | custom-call | flops 11796480 | bytes 5898240 | tf_op jit(solution)/shard_map/cross/pallas_call | solution.py:410
  85.4 0.0 collective-permute-done.5.refs_6_
  85.4 3.0 %collective-permute-done.6.refs_7_ = bf16[624,256]{1,0:T(8,128)(2,1)S(1)} collective-permute-done((bf16[624,256]{1,0:T(8,128)(2,1)}, bf16[624,256]{1,0:T(8,128)(2,1)S(1)}, u32[]{:S(2)}, u32[]{:S(2)}) %collective-permute-start.6) | collective-permute-done | bytes 319520 | tf_op jit(solution)/shard_map/ppermute | solution.py:546
  88.4 2.9 %cross.5 = bf16[4,64,256]{2,1,0:T(8,128)(2,1)S(1)} custom-call(s32[1]{0:T(128)} %bitcast.refs_0_.here_ref, bf16[768,256]{1,0:T(8,128)(2,1)S(1)} %get-tuple-element.63.refs_0_, bf16[768,256]{1,0:T(8,128)(2,1)S(1)} %get-tuple-element.64.refs_1_, bf16[768,256]{1,0:T(8,128)(2,1)S(1)} %get-tuple-element.65.refs_2_, ...), custom_call_target="tpu_custom_call" | custom-call | flops 10223616 | bytes 5111808 | tf_op jit(solution)/shard_map/cross/pallas_call | solution.py:410
  91.3 17.5 %all_to_all.20.stacks_ref = bf16[32,8,256]{2,1,0:T(8,128)(2,1)S(1)} all-to-all(bf16[32,8,256]{2,1,0:T(8,128)(2,1)S(1)} %bitcast.5), channel_id=1, replica_groups=mesh['seg'=4,'chan'=8] {'seg','chan'}, dimensions={0} | all-to-all | bytes 262144 | tf_op jit(solution)/shard_map/all_to_all | solution.py:609
  108.8 1.2 %lags.1 = f32[8,2048]{1,0:T(8,128)} custom-call(bf16[32,8,256]{2,1,0:T(8,128)(2,1)S(1)} %all_to_all.20.stacks_ref, bf16[512,512]{1,0:T(8,128)(2,1)S(1)} %copy-done.2, bf16[512,512]{1,0:T(8,128)(2,1)S(1)} %copy-done.1, bf16[1024,1024]{1,0:T(8,128)(2,1)S(1)} %copy-done), custom_call_target="tpu_custom_call" | custom-call | tf_op jit(solution)/shard_map/lags/pallas_call | solution.py:508
  (24 shorter events, 0.2 us)
Async XLA Ops:
  9.0 37.9 %all-to-all-start.2 = ((bf16[8,224,256]{2,1,0:T(8,128)(2,1)}), bf16[8,224,256]{2,1,0:T(8,128)(2,1)S(1)}, u32[]{:S(2)}, u32[]{:S(2)}) async-start(bf16[8,224,256]{2,1,0:T(8,128)(2,1)} %get-tuple-element.55), calls=%async_computation.2 | async-start | bytes 1835008 | tf_op jit(solution)/shard_map/all_to_all | solution.py:527
  35.4 39.3 %copy-start.4 = (s32[2,352]{1,0:T(2,128)S(1)}, s32[2,352]{1,0:T(2,128)}, u32[]{:S(2)}) copy-start(s32[2,352]{1,0:T(2,128)} %constant.37.clone.refs_0_) | copy-start | bytes 8452
  35.4 39.3 %copy-start.5 = (s32[2,208]{1,0:T(2,128)S(1)}, s32[2,208]{1,0:T(2,128)}, u32[]{:S(2)}) copy-start(s32[2,208]{1,0:T(2,128)} %constant.39.clone.refs_2_) | copy-start | bytes 4996
  35.4 39.3 %copy-start.6 = (s32[2,240]{1,0:T(2,128)S(1)}, s32[2,240]{1,0:T(2,128)}, u32[]{:S(2)}) copy-start(s32[2,240]{1,0:T(2,128)} %constant.38.clone.refs_1_) | copy-start | bytes 5764
  35.4 35.5 %collective-permute-start = (bf16[624,256]{1,0:T(8,128)(2,1)}, bf16[624,256]{1,0:T(8,128)(2,1)S(1)}, u32[]{:S(2)}, u32[]{:S(2)}) collective-permute-start(bf16[624,256]{1,0:T(8,128)(2,1)} %get-tuple-element.50), channel_id=1, source_target_pairs={{0,4},{1,5},{2,6},{3,7},{4,0},{5,1},{6,2},{7,3},{8,12},{9,13},{10,... | collective-permute-start | bytes 958472 | tf_op jit(solution)/shard_map/ppermute | solution.py:546
  38.4 32.5 %collective-permute-start.1 = (bf16[624,256]{1,0:T(8,128)(2,1)}, bf16[624,256]{1,0:T(8,128)(2,1)S(1)}, u32[]{:S(2)}, u32[]{:S(2)}) collective-permute-start(bf16[624,256]{1,0:T(8,128)(2,1)} %get-tuple-element.51), channel_id=1, source_target_pairs={{0,1},{1,2},{2,3},{3,4},{4,5},{5,6},{6,7},{7,0},{8,9},{9,10},{10,1... | collective-permute-start | bytes 958472 | tf_op jit(solution)/shard_map/ppermute | solution.py:546
  39.8 39.0 %collective-permute-start.2 = (bf16[624,256]{1,0:T(8,128)(2,1)}, bf16[624,256]{1,0:T(8,128)(2,1)S(1)}, u32[]{:S(2)}, u32[]{:S(2)}) collective-permute-start(bf16[624,256]{1,0:T(8,128)(2,1)} %get-tuple-element.52), channel_id=1, source_target_pairs={{0,7},{1,0},{2,1},{3,2},{4,3},{5,4},{6,5},{7,6},{8,15},{9,8},{10,9... | collective-permute-start | bytes 958472 | tf_op jit(solution)/shard_map/ppermute | solution.py:546
  43.1 39.0 %collective-permute-start.3 = (bf16[624,256]{1,0:T(8,128)(2,1)}, bf16[624,256]{1,0:T(8,128)(2,1)S(1)}, u32[]{:S(2)}, u32[]{:S(2)}) collective-permute-start(bf16[624,256]{1,0:T(8,128)(2,1)} %get-tuple-element.53), channel_id=1, source_target_pairs={{0,3},{1,4},{2,5},{3,6},{4,7},{5,0},{6,1},{7,2},{8,11},{9,12},{10,... | collective-permute-start | bytes 958472 | tf_op jit(solution)/shard_map/ppermute | solution.py:546
  43.1 39.0 %collective-permute-start.4 = (bf16[624,256]{1,0:T(8,128)(2,1)}, bf16[624,256]{1,0:T(8,128)(2,1)S(1)}, u32[]{:S(2)}, u32[]{:S(2)}) collective-permute-start(bf16[624,256]{1,0:T(8,128)(2,1)} %get-tuple-element.54), channel_id=1, source_target_pairs={{0,5},{1,6},{2,7},{3,0},{4,1},{5,2},{6,3},{7,4},{8,13},{9,14},{10,... | collective-permute-start | bytes 958472 | tf_op jit(solution)/shard_map/ppermute | solution.py:546
  48.8 0.7 copy-start.7
  49.6 32.5 %copy-start.3 = (bf16[624,256]{1,0:T(8,128)(2,1)S(1)}, bf16[624,256]{1,0:T(8,128)(2,1)}, u32[]{:S(2)}) copy-start(bf16[624,256]{1,0:T(8,128)(2,1)} %get-tuple-element.49.refs_0_) | copy-start | bytes 958468
  49.6 32.5 %copy-start.8 = (bf16[8,64,256]{2,1,0:T(8,128)(2,1)S(1)}, bf16[8,64,256]{2,1,0:T(8,128)(2,1)}, u32[]{:S(2)}) copy-start(bf16[8,64,256]{2,1,0:T(8,128)(2,1)} %copy-done.7) | copy-start | bytes 786436
  70.9 14.5 %collective-permute-start.5 = (bf16[624,256]{1,0:T(8,128)(2,1)}, bf16[624,256]{1,0:T(8,128)(2,1)S(1)}, u32[]{:S(2)}, u32[]{:S(2)}) collective-permute-start(bf16[624,256]{1,0:T(8,128)(2,1)} %get-tuple-element.71), channel_id=1, source_target_pairs={{0,2},{1,3},{2,4},{3,5},{4,6},{5,7},{6,0},{7,1},{8,10},{9,11},{10,... | collective-permute-start | bytes 958472 | tf_op jit(solution)/shard_map/ppermute | solution.py:546
  70.9 17.5 %collective-permute-start.6 = (bf16[624,256]{1,0:T(8,128)(2,1)}, bf16[624,256]{1,0:T(8,128)(2,1)S(1)}, u32[]{:S(2)}, u32[]{:S(2)}) collective-permute-start(bf16[624,256]{1,0:T(8,128)(2,1)} %get-tuple-element.72), channel_id=1, source_target_pairs={{0,6},{1,7},{2,0},{3,1},{4,2},{5,3},{6,4},{7,5},{8,14},{9,15},{10,... | collective-permute-start | bytes 958472 | tf_op jit(solution)/shard_map/ppermute | solution.py:546
  88.4 20.5 %copy-start = (bf16[1024,1024]{1,0:T(8,128)(2,1)S(1)}, bf16[1024,1024]{1,0:T(8,128)(2,1)}, u32[]{:S(2)}) copy-start(bf16[1024,1024]{1,0:T(8,128)(2,1)} %constant.42.clone.odd_ref) | copy-start | bytes 6291460
  88.4 20.5 %copy-start.1 = (bf16[512,512]{1,0:T(8,128)(2,1)S(1)}, bf16[512,512]{1,0:T(8,128)(2,1)}, u32[]{:S(2)}) copy-start(bf16[512,512]{1,0:T(8,128)(2,1)} %constant.41.clone.two_ref) | copy-start | bytes 1572868
  88.4 20.5 %copy-start.2 = (bf16[512,512]{1,0:T(8,128)(2,1)S(1)}, bf16[512,512]{1,0:T(8,128)(2,1)}, u32[]{:S(2)}) copy-start(bf16[512,512]{1,0:T(8,128)(2,1)} %constant.40.clone.zero_ref) | copy-start | bytes 1572868
where the time goes:
time: 110 us
  Pallas kernels  39.5 us (36%)
  waiting for transfers between devices  27.6 us (25%)
  starting transfers between devices  22.6 us (21%)
  blocking collectives  17.5 us (16%)
  between operations  1.27 us (1%)
    pallas_call x2, Pallas kernels, spectra(): pl.pallas_call(functools.partial(spectra_kernel, relative, with_meta, kep...  28.1 us
    ppermute x7, waiting for transfers between devices, sent_along(): lax.ppermute(second[shift], 'chan', [(i, (i + shift) % count) for i in ra...  27.6 us
    all_to_all x1, blocking collectives, per_device(): lax.all_to_all(stacks, ('seg', 'chan'), split_axis=0, concat_axis=0, tile...  17.5 us
    ppermute x7, starting transfers between devices, sent_along(): lax.ppermute(second[shift], 'chan', [(i, (i + shift) % count) for i in ra...  15.3 us
    pallas_call x3, Pallas kernels, cross(): pl.pallas_call(functools.partial(cross_kernel, plan), in_specs=[pl.BlockS...  8.91 us
    all_to_all x1, starting transfers between devices, sent_along(): lax.all_to_all(first, 'chan', split_axis=0, concat_axis=0, tiled=True)  7.3 us
  transfers between devices with their start and end apart: 8, of which 3 were waited for; matrix products, arithmetic and copies ran while one was open for 1% of the time, Pallas kernels for 24%

commit v1 on v0

--- a/solution.py
+++ b/solution.py
@@ -128,10 +128,11 @@
     f32, bf16 = jnp.float32, jnp.bfloat16
     refs = list(refs)
     here_ref = refs.pop(0) if relative else None
-    x_any, mask_ref, owner_ref, bins_ref, even_any, odd_any, band_any = refs[:7]
-    x_refs, even_ref, odd_ref, band_ref, x_came, arrived, plus, minus, v, ab, early, others, windows = refs[-13:]
-    out_refs = refs[7:-14] if relative else refs[7:-13]
-    head = refs[-14] if relative else out_refs[0]
+    x_any, mask_any, owner_any, bins_any, even_any, odd_any, band_any = refs[:7]
+    x_refs, even_ref, odd_ref, band_ref, mask_ref, owner_ref, bins_ref = refs[-16:-9]
+    x_came, arrived, plus, minus, v, ab, early, others, windows = refs[-9:]
+    out_refs = refs[7:-17] if relative else refs[7:-16]
+    head = refs[-17] if relative else out_refs[0]
     spares = out_refs[1 - len(TIERS):] if kept < PAIR else []
     step, steps = pl.program_id(0), pl.num_programs(0)
     first = step == 0
@@ -139,6 +140,9 @@
     slot = 0 if alone else lax.rem(step, 2)
     at_first = (lambda act: act()) if alone else pl.when(first)
     moves = ((even_any, even_ref), (odd_any, odd_ref), (band_any, band_ref))
+    moves += ((mask_any, mask_ref),)
+    if with_meta:
+        moves += ((owner_any, owner_ref), (bins_any, bins_ref))
     copies = [pltpu.make_async_copy(source, into, arrived.at[i]) for i, (source, into) in enumerate(moves)]
 
     def trace_copy(block, slot):
@@ -150,6 +154,11 @@
         trace_copy(0, 0).start()
         for copy in copies:
             copy.start()
+
+    @at_first
+    def table_waits():
+        for copy in copies:
+            copy.wait()
 
     mask = mask_ref[...].astype(f32)
     if kept < PAIR:
@@ -165,11 +174,6 @@
         @pl.when(step + 1 < steps)
         def ahead():
             trace_copy(step + 1, 1 - slot).start()
-
-    @at_first
-    def table_waits():
-        for copy in copies:
-            copy.wait()
 
     x_ref = x_refs.at[slot]
     x = [x_ref[:, m * QUARTER:(m + 1) * QUARTER].astype(f32) for m in range(FOLD)]
@@ -254,15 +258,14 @@
 def spectra(traces, mask, owners, bins, first_row, rows, block, kept, here=None, with_meta=False):
     relative = here is not None
     tables = [jnp.asarray(table) for table in forward_tables() + (band_table(),)]
-    whole = lambda array: pl.BlockSpec(array.shape, lambda i, *_: (0, 0))
     in_place = pl.BlockSpec(memory_space=pl.ANY)
     f32, bf16 = jnp.float32, jnp.bfloat16
     pairs = block // PAIR
     scratch = [
         pltpu.VMEM((2, block, NT), bf16),
-    ] + [pltpu.VMEM(table.shape, bf16) for table in tables] + [
+    ] + [pltpu.VMEM(array.shape, array.dtype) for array in (*tables, mask, owners, bins)] + [
         pltpu.SemaphoreType.DMA((2,)),
-        pltpu.SemaphoreType.DMA((3,)),
+        pltpu.SemaphoreType.DMA((6,)),
     ]
     scratch += [pltpu.VMEM((terms * block, EIGHTH), bf16) for terms in (2, 2, 4)]
     scratch += [pltpu.VMEM((4 * block, QUARTER), bf16)]
@@ -284,7 +287,7 @@
         grid_spec=pltpu.PrefetchScalarGridSpec(
             num_scalar_prefetch=1 if relative else 0,
             grid=(rows // block,),
-            in_specs=[in_place, whole(mask), whole(owners), whole(bins)] + [in_place] * len(tables),
+            in_specs=[in_place] * (4 + len(tables)),
             out_specs=out_specs,
             scratch_shapes=scratch,
         ),

time: 110 us -> 109 us (level)
  Pallas kernels: 39.5 us -> 38.4 us
    pallas_call x2, Pallas kernels: 28.1 us -> 27 us  [spectra(): pl.pallas_call(functools.partial(spectra_kernel, relative, with_meta, kep...]
  transfers between devices with their start and end apart: 8 -> 8, of which waited for: 3 -> 4; matrix products, arithmetic and copies ran while one was open for 1% -> 1% of each run, Pallas kernels for 24% -> 24%
where the time goes in v1:
time: 109 us
  Pallas kernels  38.4 us (35%)
  waiting for transfers between devices  28.5 us (26%)
  starting transfers between devices  22.6 us (21%)
  blocking collectives  16.6 us (15%)
  between operations  1.27 us (1%)
    ppermute x7, waiting for transfers between devices, sent_along(): lax.ppermute(second[shift], 'chan', [(i, (i + shift) % count) for i in ra...  28.3 us
    pallas_call x2, Pallas kernels, spectra(): pl.pallas_call(functools.partial(spectra_kernel, relative, with_meta, kep...  27 us
    all_to_all x1, blocking collectives, per_device(): lax.all_to_all(stacks, ('seg', 'chan'), split_axis=0, concat_axis=0, tile...  16.6 us
    ppermute x7, starting transfers between devices, sent_along(): lax.ppermute(second[shift], 'chan', [(i, (i + shift) % count) for i in ra...  15.4 us
    pallas_call x3, Pallas kernels, cross(): pl.pallas_call(functools.partial(cross_kernel, plan), in_specs=[pl.BlockS...  8.91 us
    all_to_all x1, starting transfers between devices, sent_along(): lax.all_to_all(first, 'chan', split_axis=0, concat_axis=0, tiled=True)  7.29 us
  transfers between devices with their start and end apart: 8, of which 4 were waited for; matrix products, arithmetic and copies ran while one was open for 1% of the time, Pallas kernels for 24%

profile of v1, /device:TPU:0, one launch (start us, length us, event | category | flops | bytes accessed | tf_op | source)
XLA Modules:
  0.0 108.9 jit_solution(13276714078471341371)
XLA Ops:
  0.0 8.4 %spectra.3 = (bf16[8,224,256]{2,1,0:T(8,128)(2,1)}, bf16[8,16,256]{2,1,0:T(8,128)(2,1)S(1)}, bf16[8,32,256]{2,1,0:T(8,128)(2,1)S(1)}) custom-call(bf16[1024,4096]{1,0:T(8,128)(2,1)} %bitcast.6, s32[1,128]{1,0:T(1,128)} %bitcast.8, s32[1,64]{1,0:T(1,128)} %bitcast.10, s32[1,64]{1,0:T(1,128)} %refs_3_.1, bf16[2,512,512]{2,1,0:T(8,128)(2,1)} %constant.34.clone.refs_5_.refs_4_, ...), custom_call_target="tpu_custom_call" | custom-call | flops 3758096384 | bytes 11534336 | tf_op jit(solution)/shard_map/spectra/pallas_call | solution.py:285
  8.5 7.3 %all-to-all-start.2 = ((bf16[8,224,256]{2,1,0:T(8,128)(2,1)}), bf16[8,224,256]{2,1,0:T(8,128)(2,1)S(1)}, u32[]{:S(2)}, u32[]{:S(2)}) async-start(bf16[8,224,256]{2,1,0:T(8,128)(2,1)} %get-tuple-element.55), calls=%async_computation.2 | async-start | bytes 1835008 | tf_op jit(solution)/shard_map/all_to_all | solution.py:530
  15.8 18.5 %spectra.2 = (bf16[624,256]{1,0:T(8,128)(2,1)}, bf16[624,256]{1,0:T(8,128)(2,1)}, bf16[624,256]{1,0:T(8,128)(2,1)}, bf16[624,256]{1,0:T(8,128)(2,1)}, bf16[624,2...) custom-call(s32[1]{0:T(128)} %bitcast.refs_0_.here_ref, ...), custom_call_target="tpu_custom_call" | custom-call | flops 11274289152 | bytes 17825792 | tf_op jit(solution)/shard_map/spectra/pallas_call | solution.py:285
  34.3 0.0 copy-start.4
  34.3 0.0 copy-start.5
  34.3 0.0 copy-start.6
  34.3 3.0 %collective-permute-start = (bf16[624,256]{1,0:T(8,128)(2,1)}, bf16[624,256]{1,0:T(8,128)(2,1)S(1)}, u32[]{:S(2)}, u32[]{:S(2)}) collective-permute-start(bf16[624,256]{1,0:T(8,128)(2,1)} %get-tuple-element.50), channel_id=1, source_target_pairs={{0,4},{1,5},{2,6},{3,7},{4,0},{5,1},{6,2},{7,3},{8,12},{9,13},{10,... | collective-permute-start | bytes 958472 | tf_op jit(solution)/shard_map/ppermute | solution.py:549
  37.3 1.5 %collective-permute-start.1 = (bf16[624,256]{1,0:T(8,128)(2,1)}, bf16[624,256]{1,0:T(8,128)(2,1)S(1)}, u32[]{:S(2)}, u32[]{:S(2)}) collective-permute-start(bf16[624,256]{1,0:T(8,128)(2,1)} %get-tuple-element.51), channel_id=1, source_target_pairs={{0,1},{1,2},{2,3},{3,4},{4,5},{5,6},{6,7},{7,0},{8,9},{9,10},{10,1... | collective-permute-start | bytes 958472 | tf_op jit(solution)/shard_map/ppermute | solution.py:549
  38.8 3.3 %collective-permute-start.2 = (bf16[624,256]{1,0:T(8,128)(2,1)}, bf16[624,256]{1,0:T(8,128)(2,1)S(1)}, u32[]{:S(2)}, u32[]{:S(2)}) collective-permute-start(bf16[624,256]{1,0:T(8,128)(2,1)} %get-tuple-element.52), channel_id=1, source_target_pairs={{0,7},{1,0},{2,1},{3,2},{4,3},{5,4},{6,5},{7,6},{8,15},{9,8},{10,9... | collective-permute-start | bytes 958472 | tf_op jit(solution)/shard_map/ppermute | solution.py:549
  42.0 3.8 %collective-permute-start.4 = (bf16[624,256]{1,0:T(8,128)(2,1)}, bf16[624,256]{1,0:T(8,128)(2,1)S(1)}, u32[]{:S(2)}, u32[]{:S(2)}) collective-permute-start(bf16[624,256]{1,0:T(8,128)(2,1)} %get-tuple-element.54), channel_id=1, source_target_pairs={{0,5},{1,6},{2,7},{3,0},{4,1},{5,2},{6,3},{7,4},{8,13},{9,14},{10,... | collective-permute-start | bytes 958472 | tf_op jit(solution)/shard_map/ppermute | solution.py:549
  45.8 0.1 all-to-all-done.2.meta_ref.refs_0_
  46.0 0.1 fusion
  46.1 0.6 reduce_max.9
  47.9 0.7 copy-done.7
  48.7 22.0 %collective-permute-done.refs_1_ = bf16[624,256]{1,0:T(8,128)(2,1)S(1)} collective-permute-done((bf16[624,256]{1,0:T(8,128)(2,1)}, bf16[624,256]{1,0:T(8,128)(2,1)S(1)}, u32[]{:S(2)}, u32[]{:S(2)}) %collective-permute-start) | collective-permute-done | bytes 319520 | tf_op jit(solution)/shard_map/ppermute | solution.py:549
  70.7 3.8 %collective-permute-start.6 = (bf16[624,256]{1,0:T(8,128)(2,1)}, bf16[624,256]{1,0:T(8,128)(2,1)S(1)}, u32[]{:S(2)}, u32[]{:S(2)}) collective-permute-start(bf16[624,256]{1,0:T(8,128)(2,1)} %get-tuple-element.72), channel_id=1, source_target_pairs={{0,6},{1,7},{2,0},{3,1},{4,2},{5,3},{6,4},{7,5},{8,14},{9,15},{10,... | collective-permute-start | bytes 958472 | tf_op jit(solution)/shard_map/ppermute | solution.py:549
  74.5 1.3 %weights.1 = (f32[8,352]{1,0:T(8,128)S(1)}, f32[8,240]{1,0:T(8,128)S(1)}, f32[8,208]{1,0:T(8,128)S(1)}, bf16[8,256,256]{2,1,0:T(8,128)(2,1)S(1)}) custom-call(s32[1]{0:T(128)} %bitcast.refs_0_.here_ref, bf16[8,224,256]{2,1,0:T(8,128)(2,1)S(1)} %all-to-all-done.2.meta_ref.refs_0_, s32[2,352]{1,0:T(2,128)S(1)} %copy-done.4, s32[2,240]{1,0:T(2,128)S(1)} %copy-done.6, ...), custom_call_target="tpu_custom_call" | custom-call | tf_op jit(solution)/shard_map/weights/pallas_call | solution.py:468
  75.9 2.7 %cross.3.refs_10_ = f32[64,256]{1,0:T(8,128)S(1)} custom-call(s32[1]{0:T(128)} %bitcast.refs_0_.here_ref, bf16[8,224,256]{2,1,0:T(8,128)(2,1)S(1)} %all-to-all-done.2.meta_ref.refs_0_, bf16[8,64,256]{2,1,0:T(8,128)(2,1)} %copy-done.7, bf16[8,128,256]{2,1,0:T(8,128)(2,1)S(1)} %get-tuple-element.76.refs_2_.refs_7_.refs_9_, ...), custom_call_target="tpu_custom_call" | custom-call | flops 5767168 | bytes 2883584 | tf_op jit(solution)/shard_map/cross/pallas_call | solution.py:413
  78.6 2.7 %collective-permute-done.3.refs_4_ = bf16[624,256]{1,0:T(8,128)(2,1)S(1)} collective-permute-done((bf16[624,256]{1,0:T(8,128)(2,1)}, bf16[624,256]{1,0:T(8,128)(2,1)S(1)}, u32[]{:S(2)}, u32[]{:S(2)}) %collective-permute-start.3) | collective-permute-done | bytes 319520 | tf_op jit(solution)/shard_map/ppermute | solution.py:549
  81.4 3.2 %cross.4 = (f32[64,256]{1,0:T(8,128)S(1)}, bf16[768,256]{1,0:T(8,128)(2,1)S(1)}, bf16[768,256]{1,0:T(8,128)(2,1)S(1)}, bf16[768,256]{1,0:T(8,128)(2,1)S(1)}, bf1...) custom-call(s32[1]{0:T(128)} %bitcast.refs_0_.here_ref, ...), custom_call_target="tpu_custom_call" | custom-call | flops 11796480 | bytes 5898240 | tf_op jit(solution)/shard_map/cross/pallas_call | solution.py:413
  84.6 3.5 %collective-permute-done.6.refs_7_ = bf16[624,256]{1,0:T(8,128)(2,1)S(1)} collective-permute-done((bf16[624,256]{1,0:T(8,128)(2,1)}, bf16[624,256]{1,0:T(8,128)(2,1)S(1)}, u32[]{:S(2)}, u32[]{:S(2)}) %collective-permute-start.6) | collective-permute-done | bytes 319520 | tf_op jit(solution)/shard_map/ppermute | solution.py:549
  88.2 2.9 %cross.5 = bf16[4,64,256]{2,1,0:T(8,128)(2,1)S(1)} custom-call(s32[1]{0:T(128)} %bitcast.refs_0_.here_ref, bf16[768,256]{1,0:T(8,128)(2,1)S(1)} %get-tuple-element.63.refs_0_, bf16[768,256]{1,0:T(8,128)(2,1)S(1)} %get-tuple-element.64.refs_1_, bf16[768,256]{1,0:T(8,128)(2,1)S(1)} %get-tuple-element.65.refs_2_, ...), custom_call_target="tpu_custom_call" | custom-call | flops 10223616 | bytes 5111808 | tf_op jit(solution)/shard_map/cross/pallas_call | solution.py:413
  91.1 16.6 %all_to_all.20.stacks_ref = bf16[32,8,256]{2,1,0:T(8,128)(2,1)S(1)} all-to-all(bf16[32,8,256]{2,1,0:T(8,128)(2,1)S(1)} %bitcast.5), channel_id=1, replica_groups=mesh['seg'=4,'chan'=8] {'seg','chan'}, dimensions={0} | all-to-all | bytes 262144 | tf_op jit(solution)/shard_map/all_to_all | solution.py:612
  107.8 1.2 %lags.1 = f32[8,2048]{1,0:T(8,128)} custom-call(bf16[32,8,256]{2,1,0:T(8,128)(2,1)S(1)} %all_to_all.20.stacks_ref, bf16[512,512]{1,0:T(8,128)(2,1)S(1)} %copy-done.2, bf16[512,512]{1,0:T(8,128)(2,1)S(1)} %copy-done.1, bf16[1024,1024]{1,0:T(8,128)(2,1)S(1)} %copy-done), custom_call_target="tpu_custom_call" | custom-call | tf_op jit(solution)/shard_map/lags/pallas_call | solution.py:511
  (24 shorter events, 0.2 us)
Async XLA Ops:
  8.5 37.5 %all-to-all-start.2 = ((bf16[8,224,256]{2,1,0:T(8,128)(2,1)}), bf16[8,224,256]{2,1,0:T(8,128)(2,1)S(1)}, u32[]{:S(2)}, u32[]{:S(2)}) async-start(bf16[8,224,256]{2,1,0:T(8,128)(2,1)} %get-tuple-element.55), calls=%async_computation.2 | async-start | bytes 1835008 | tf_op jit(solution)/shard_map/all_to_all | solution.py:530
  34.3 40.3 %copy-start.4 = (s32[2,352]{1,0:T(2,128)S(1)}, s32[2,352]{1,0:T(2,128)}, u32[]{:S(2)}) copy-start(s32[2,352]{1,0:T(2,128)} %constant.37.clone.refs_0_) | copy-start | bytes 8452
  34.3 40.3 %copy-start.5 = (s32[2,208]{1,0:T(2,128)S(1)}, s32[2,208]{1,0:T(2,128)}, u32[]{:S(2)}) copy-start(s32[2,208]{1,0:T(2,128)} %constant.39.clone.refs_2_) | copy-start | bytes 4996
  34.3 40.2 %copy-start.6 = (s32[2,240]{1,0:T(2,128)S(1)}, s32[2,240]{1,0:T(2,128)}, u32[]{:S(2)}) copy-start(s32[2,240]{1,0:T(2,128)} %constant.38.clone.refs_1_) | copy-start | bytes 5764
  34.3 36.4 %collective-permute-start = (bf16[624,256]{1,0:T(8,128)(2,1)}, bf16[624,256]{1,0:T(8,128)(2,1)S(1)}, u32[]{:S(2)}, u32[]{:S(2)}) collective-permute-start(bf16[624,256]{1,0:T(8,128)(2,1)} %get-tuple-element.50), channel_id=1, source_target_pairs={{0,4},{1,5},{2,6},{3,7},{4,0},{5,1},{6,2},{7,3},{8,12},{9,13},{10,... | collective-permute-start | bytes 958472 | tf_op jit(solution)/shard_map/ppermute | solution.py:549
  37.3 33.4 %collective-permute-start.1 = (bf16[624,256]{1,0:T(8,128)(2,1)}, bf16[624,256]{1,0:T(8,128)(2,1)S(1)}, u32[]{:S(2)}, u32[]{:S(2)}) collective-permute-start(bf16[624,256]{1,0:T(8,128)(2,1)} %get-tuple-element.51), channel_id=1, source_target_pairs={{0,1},{1,2},{2,3},{3,4},{4,5},{5,6},{6,7},{7,0},{8,9},{9,10},{10,1... | collective-permute-start | bytes 958472 | tf_op jit(solution)/shard_map/ppermute | solution.py:549
  38.8 39.9 %collective-permute-start.2 = (bf16[624,256]{1,0:T(8,128)(2,1)}, bf16[624,256]{1,0:T(8,128)(2,1)S(1)}, u32[]{:S(2)}, u32[]{:S(2)}) collective-permute-start(bf16[624,256]{1,0:T(8,128)(2,1)} %get-tuple-element.52), channel_id=1, source_target_pairs={{0,7},{1,0},{2,1},{3,2},{4,3},{5,4},{6,5},{7,6},{8,15},{9,8},{10,9... | collective-permute-start | bytes 958472 | tf_op jit(solution)/shard_map/ppermute | solution.py:549
  42.0 39.4 %collective-permute-start.3 = (bf16[624,256]{1,0:T(8,128)(2,1)}, bf16[624,256]{1,0:T(8,128)(2,1)S(1)}, u32[]{:S(2)}, u32[]{:S(2)}) collective-permute-start(bf16[624,256]{1,0:T(8,128)(2,1)} %get-tuple-element.53), channel_id=1, source_target_pairs={{0,3},{1,4},{2,5},{3,6},{4,7},{5,0},{6,1},{7,2},{8,11},{9,12},{10,... | collective-permute-start | bytes 958472 | tf_op jit(solution)/shard_map/ppermute | solution.py:549
  42.0 39.4 %collective-permute-start.4 = (bf16[624,256]{1,0:T(8,128)(2,1)}, bf16[624,256]{1,0:T(8,128)(2,1)S(1)}, u32[]{:S(2)}, u32[]{:S(2)}) collective-permute-start(bf16[624,256]{1,0:T(8,128)(2,1)} %get-tuple-element.54), channel_id=1, source_target_pairs={{0,5},{1,6},{2,7},{3,0},{4,1},{5,2},{6,3},{7,4},{8,13},{9,14},{10,... | collective-permute-start | bytes 958472 | tf_op jit(solution)/shard_map/ppermute | solution.py:549
  47.9 0.7 copy-start.7
  48.7 32.7 %copy-start.3 = (bf16[624,256]{1,0:T(8,128)(2,1)S(1)}, bf16[624,256]{1,0:T(8,128)(2,1)}, u32[]{:S(2)}) copy-start(bf16[624,256]{1,0:T(8,128)(2,1)} %get-tuple-element.49.refs_0_) | copy-start | bytes 958468
  48.7 32.7 %copy-start.8 = (bf16[8,64,256]{2,1,0:T(8,128)(2,1)S(1)}, bf16[8,64,256]{2,1,0:T(8,128)(2,1)}, u32[]{:S(2)}) copy-start(bf16[8,64,256]{2,1,0:T(8,128)(2,1)} %copy-done.7) | copy-start | bytes 786436
  70.7 13.9 %collective-permute-start.5 = (bf16[624,256]{1,0:T(8,128)(2,1)}, bf16[624,256]{1,0:T(8,128)(2,1)S(1)}, u32[]{:S(2)}, u32[]{:S(2)}) collective-permute-start(bf16[624,256]{1,0:T(8,128)(2,1)} %get-tuple-element.71), channel_id=1, source_target_pairs={{0,2},{1,3},{2,4},{3,5},{4,6},{5,7},{6,0},{7,1},{8,10},{9,11},{10,... | collective-permute-start | bytes 958472 | tf_op jit(solution)/shard_map/ppermute | solution.py:549
  70.7 17.5 %collective-permute-start.6 = (bf16[624,256]{1,0:T(8,128)(2,1)}, bf16[624,256]{1,0:T(8,128)(2,1)S(1)}, u32[]{:S(2)}, u32[]{:S(2)}) collective-permute-start(bf16[624,256]{1,0:T(8,128)(2,1)} %get-tuple-element.72), channel_id=1, source_target_pairs={{0,6},{1,7},{2,0},{3,1},{4,2},{5,3},{6,4},{7,5},{8,14},{9,15},{10,... | collective-permute-start | bytes 958472 | tf_op jit(solution)/shard_map/ppermute | solution.py:549
  88.2 19.6 %copy-start = (bf16[1024,1024]{1,0:T(8,128)(2,1)S(1)}, bf16[1024,1024]{1,0:T(8,128)(2,1)}, u32[]{:S(2)}) copy-start(bf16[1024,1024]{1,0:T(8,128)(2,1)} %constant.42.clone.odd_ref) | copy-start | bytes 6291460
  88.2 19.6 %copy-start.1 = (bf16[512,512]{1,0:T(8,128)(2,1)S(1)}, bf16[512,512]{1,0:T(8,128)(2,1)}, u32[]{:S(2)}) copy-start(bf16[512,512]{1,0:T(8,128)(2,1)} %constant.41.clone.two_ref) | copy-start | bytes 1572868
  88.2 19.6 %copy-start.2 = (bf16[512,512]{1,0:T(8,128)(2,1)S(1)}, bf16[512,512]{1,0:T(8,128)(2,1)}, u32[]{:S(2)}) copy-start(bf16[512,512]{1,0:T(8,128)(2,1)} %constant.40.clone.zero_ref) | copy-start | bytes 1572868
